TPU v7x, 32 devices: a whole 2x2x4 slice. The times are simulated.
32 devices in a mesh: groups: 2 (over y), ep: 4 (over z), tp: 4 (over x, core).
Axes of the slice: x: 2, y: 2, z: 4, core: 2. Of those that a mesh axis runs over, the one named last changes fastest.
Arguments:
- normed: bfloat16 [32, 4096], P(('groups', 'ep'), 'tp'), parts along dimension 0, may hold values from -6 to 6
- residual: bfloat16 [32, 4096], P(('groups', 'ep'), 'tp'), parts along dimension 0, may hold values from -4 to 4
- expert_ids: int32 [32, 2], P(('groups', 'ep')), parts along dimension 0, may hold values from 0 to 3, all different within a row; in each aligned block of 4 rows (0 to 3, 4 to 7, ...) at most 3 rows name the same one
- route_weight: float32 [32, 2], P(('groups', 'ep')), parts along dimension 0, may hold values from 0.05 to 1
- w_gate: bfloat16 [4, 4096, 1024], P('ep', 'tp'), may hold values from -0.09375 to 0.09375
- w_up: bfloat16 [4, 4096, 1024], P('ep', 'tp'), may hold values from -0.09375 to 0.09375
- w_down: bfloat16 [4, 1024, 4096], P('ep', None, 'tp'), may hold values from -0.1875 to 0.1875
- w_kv: bfloat16 [4096, 1024], P('tp'), may hold values from -0.09375 to 0.09375
- key_gain: float32 [128], replicated, may hold values from 0.1 to 1.9
- prefill_kv: bfloat16 [8, 4, 80, 1024], P(('groups', 'ep'), None, None, 'tp'), parts along dimension 0
- order: int32 [8, 4], P(('groups', 'ep')), parts along dimension 0, may hold values from 0 to 3, each once within a row
- lengths: int32 [32], P(('groups', 'ep', 'tp')), parts along dimension 0, may hold values from 2 to 80
- queries: bfloat16 [32, 8192], P(('groups', 'ep', 'tp')), parts along dimension 0
Outputs:
- hidden_state: bfloat16 [32, 4096], P(('groups', 'ep'), 'tp'), parts along dimension 0
- attention: bfloat16 [32, 8192], P(('groups', 'ep', 'tp')), parts along dimension 0
There are 2 independent parts, one for each index of `groups`. A program takes and returns all parts, laid end to end along the dimension named above; an argument that names none is the same for every part. Nothing has to cross between parts.
Inputs may be any that keep to these rules, and one draw needn't show every extreme that they name: `expert_ids`: in the rows of one decode rank (aligned blocks of 4 rows), no expert is named by more than 3 rows; some expert is named by exactly 3 of them in some blocks. Each row names 2 different experts. `order`: each row is a permutation of 0 to 3.
All inputs are finite; a program needn't handle non-finite values.
Results may differ from a plain program's by a relative error of at most 0.0053.
Values may be sent and summed in bfloat16 or wider, within the bound.
A program may use at most 64 MiB of HBM per device.

v0:
```python
import jax
import jax.numpy as jnp
from jax import lax
from jax.sharding import PartitionSpec as P

QH = 64
KVH = 4
HD = 128


def rotary_key(key_rows, positions):
    half_size = HD // 2
    exponent = jnp.arange(half_size, dtype=jnp.float32) * (-2.0 / HD)
    frequency = jnp.power(jnp.float32(1000000.0), exponent)
    angles = positions.astype(jnp.float32)[:, None, None] * frequency[None, None, :]
    cosine = jnp.cos(angles)
    sine_part = jnp.sin(angles)
    leading = key_rows[..., :half_size]
    trailing = key_rows[..., half_size:]
    return jnp.concatenate(
        [leading * cosine - trailing * sine_part, trailing * cosine + leading * sine_part], axis=-1
    )


def attend(query_rows, cache, fresh, lengths, key_gain):
    rows = query_rows.shape[0]
    ctx = cache.shape[1]
    inv_root = 1.0 / jnp.sqrt(jnp.float32(HD))
    parts = fresh.reshape(rows, KVH, 2, HD)
    new_key = parts[:, :, 0].astype(jnp.float32)
    factor = lax.rsqrt(jnp.mean(new_key * new_key, axis=-1, keepdims=True) + 1e-06)
    new_key = rotary_key(new_key * factor * key_gain, lengths).astype(jnp.bfloat16)
    new_value = parts[:, :, 1]
    stored = cache.reshape(rows, ctx, KVH, 2, HD)
    keys = stored[:, :, :, 0]
    values = stored[:, :, :, 1]
    query = query_rows.reshape(rows, KVH, QH // KVH, HD)
    scores = (
        jnp.einsum("rgqd,rcgd->rgqc", query, keys, preferred_element_type=jnp.float32) * inv_root
    )
    fresh_score = (
        jnp.einsum("rgqd,rgd->rgq", query, new_key, preferred_element_type=jnp.float32) * inv_root
    )
    live = (jnp.arange(ctx, dtype=jnp.int32)[None, :] < lengths[:, None])[:, None, None, :]
    scores = jnp.where(live, scores, jnp.float32(-1e30))
    top = jnp.maximum(jnp.max(scores, axis=-1), fresh_score)
    weights = jnp.where(live, jnp.exp(scores - top[..., None]), jnp.float32(0.0))
    fresh_weight = jnp.exp(fresh_score - top)
    total = jnp.sum(weights, axis=-1) + fresh_weight
    probs = (weights / total[..., None]).astype(jnp.bfloat16)
    fresh_prob = (fresh_weight / total).astype(jnp.bfloat16)
    out = jnp.einsum("rgqc,rcgd->rgqd", probs, values, preferred_element_type=jnp.float32)
    out = (
        out
        + fresh_prob.astype(jnp.float32)[..., None] * new_value.astype(jnp.float32)[:, :, None, :]
    )
    return out.reshape(rows, QH * HD).astype(jnp.bfloat16)


def on_device(
    normed,
    residual,
    expert_ids,
    route_weight,
    w_gate,
    w_up,
    w_down,
    w_kv,
    key_gain,
    prefill_kv,
    order,
    lengths,
    queries,
):
    ep_count = lax.axis_size("ep")
    rows_ep, width = normed.shape
    chosen = expert_ids.shape[1]
    capacity = 2 * rows_ep * chosen // ep_count - 1
    flat = expert_ids.reshape(-1)
    onehot = (flat[:, None] == jnp.arange(ep_count, dtype=jnp.int32)[None, :]).astype(jnp.int32)
    before = jnp.cumsum(onehot, axis=0) - onehot
    slot = jnp.sum(before * onehot, axis=1)
    source = jnp.arange(rows_ep * chosen, dtype=jnp.int32) // chosen
    outgoing = (
        jnp.zeros((ep_count, capacity, width), jnp.bfloat16).at[flat, slot].set(normed[source])
    )
    received = lax.all_to_all(outgoing, "ep", split_axis=0, concat_axis=0, tiled=True)
    count = received.shape[1]
    rows = received.reshape(ep_count * count, width)
    gate = jnp.dot(rows, w_gate[0], preferred_element_type=jnp.float32)
    up = jnp.dot(rows, w_up[0], preferred_element_type=jnp.float32)
    gate, up = lax.psum((gate, up), "tp")
    inner = (jax.nn.silu(gate) * up).astype(jnp.bfloat16)
    result = jnp.dot(inner, w_down[0], preferred_element_type=jnp.float32).astype(jnp.bfloat16)
    result = result.reshape(ep_count, count, width)
    returned = lax.all_to_all(result, "ep", split_axis=0, concat_axis=0, tiled=True)
    fetched = returned[flat, slot].astype(jnp.float32).reshape(rows_ep, chosen, width)
    share = route_weight / jnp.sum(route_weight, axis=1, keepdims=True)
    mixed = jnp.sum(fetched * share[:, :, None], axis=1)
    hidden_state = (residual.astype(jnp.float32) + mixed).astype(jnp.bfloat16)
    fresh = lax.psum_scatter(
        jnp.dot(hidden_state, w_kv, preferred_element_type=jnp.float32),
        "tp",
        scatter_dimension=0,
        tiled=True,
    ).astype(jnp.bfloat16)
    arranged = jnp.take(prefill_kv[0], order[0], axis=0)
    cache = lax.all_to_all(
        lax.all_to_all(arranged, "ep", split_axis=0, concat_axis=0, tiled=True),
        "tp",
        split_axis=0,
        concat_axis=2,
        tiled=True,
    )
    attention = attend(queries, cache, fresh, lengths, key_gain)
    return (hidden_state, attention)


def solution(mesh):
    in_specs = (
        P(("groups", "ep"), "tp"),
        P(("groups", "ep"), "tp"),
        P(("groups", "ep"), None),
        P(("groups", "ep"), None),
        P("ep", "tp", None),
        P("ep", "tp", None),
        P("ep", None, "tp"),
        P("tp", None),
        P(),
        P(("groups", "ep"), None, None, "tp"),
        P(("groups", "ep"), None),
        P(("groups", "ep", "tp")),
        P(("groups", "ep", "tp"), None),
    )
    out_specs = (P(("groups", "ep"), "tp"), P(("groups", "ep", "tp"), None))
    return jax.shard_map(
        on_device, mesh=mesh, in_specs=in_specs, out_specs=out_specs, check_vma=False
    )
```

profile of v0, /device:TPU:0, one launch (start us, length us, event | category | flops | bytes accessed | tf_op | source)
XLA Modules:
  0.0 107.2 jit_solution(1601709139426358006)
XLA Ops:
  7.2 0.9 copy.34
  8.5 1.3 %gather_fusion = bf16[8,1024]{1,0:T(8,128)(2,1)S(1)} fusion(bf16[4,1024]{1,0:T(4,128)(2,1)} %param.13, s32[1024]{0:T(1024)S(1)} %pad_clamp_fusion.1), kind=kCustom, calls=%fused_computation | custom fusion | bytes 32800 | tf_op jit(solution)/shard_map/gather | solution.py:85
  9.8 1.0 scatter_fusion
  10.8 0.6 copy.36
  11.5 6.3 %all-to-all-start = ((bf16[4,3,1024]{2,1,0:T(4,128)(2,1)}), bf16[4,3,1024]{2,1,0:T(4,128)(2,1)S(1)}, u32[]{:S(2)}, u32[]{:S(2)}) async-start(bf16[4,3,1024]{2,1,0:T(4,128)(2,1)} %copy.36), calls=%async_computation | async-start | bytes 65536 | tf_op jit(solution)/shard_map/all_to_all | solution.py:87
  17.8 0.7 fusion.28
  18.5 0.7 compare_and_fusion
  19.1 0.7 reduce_sum.49
  19.8 1.5 %gather_fusion.2 = bf16[4,80,256]{2,1,0:T(8,128)(2,1)S(1)} fusion(bf16[4,80,256]{2,1,0:T(8,128)(2,1)} %bitcast.74, s32[1024]{0:T(1024)S(1)} %pad_clamp_fusion), kind=kCustom, calls=%fused_computation.2 | custom fusion | bytes 327696 | tf_op jit(solution)/shard_map/jit(_take)/gather | solution.py:107
  21.3 0.7 broadcast_select_fusion
  22.0 0.7 broadcast_divide_fusion
  23.5 1.0 fusion.2
  24.5 0.6 copy-done.1
  25.1 1.0 fusion.4
  26.2 33.0 %all-reduce.4.cloned.1.call-done = (f32[12,1024]{1,0:T(8,128)}, f32[12,1024]{1,0:T(8,128)}) async-done(((f32[12,1024]{1,0:T(8,128)}, f32[12,1024]{1,0:T(8,128)}), (f32[12,1024]{1,0:T(8,128)}, f32[12,1024]{1,0:T(8,128)})) %all-reduce.4.cloned.1.call-update) | async-done | bytes 98320 | tf_op jit(solution)/shard_map/psum | solution.py:92
  59.2 2.1 %fusion.6 = bf16[12,1024]{1,0:T(8,128)(2,1)S(1)} fusion(bf16[1,1024,1024]{2,1,0:T(8,128)(2,1)} %param.19, f32[12,1024]{1,0:T(8,128)} %get-tuple-element.2, f32[12,1024]{1,0:T(8,128)} %get-tuple-element.3), kind=kOutput, calls=%fused_computation.10 | convolution fusion | flops 25251840 | bytes 2220032 | tf_op jit(solution)/shard_map/dot_general | solution.py:94
  61.3 0.7 reshape.354
  61.9 4.6 %all-to-all-start.1 = ((bf16[4,3,1024]{2,1,0:T(4,128)(2,1)}), bf16[4,3,1024]{2,1,0:T(4,128)(2,1)S(1)}, u32[]{:S(2)}, u32[]{:S(2)}) async-start(bf16[4,3,1024]{2,1,0:T(4,128)(2,1)} %reshape.354), calls=%async_computation.1 | async-start | bytes 65536 | tf_op jit(solution)/shard_map/all_to_all | solution.py:96
  66.7 0.7 dynamic-slice
  67.4 4.8 %all-to-all-done.1 = bf16[4,3,1024]{2,1,0:T(4,128)(2,1)S(1)} async-done(((bf16[4,3,1024]{2,1,0:T(4,128)(2,1)}), bf16[4,3,1024]{2,1,0:T(4,128)(2,1)S(1)}, u32[]{:S(2)}, u32[]{:S(2)}) %all-to-all-start.1) | async-done | bytes 24608 | tf_op jit(solution)/shard_map/all_to_all | solution.py:96
  72.2 4.0 %all-to-all-start.2 = ((bf16[4,80,256]{2,1,0:T(8,128)(2,1)}), bf16[4,80,256]{2,1,0:T(8,128)(2,1)}, u32[]{:S(2)}, u32[]{:S(2)}) async-start(bf16[4,80,256]{2,1,0:T(8,128)(2,1)} %broadcast_select_fusion), calls=%async_computation.2 | async-start | bytes 327680 | tf_op jit(solution)/shard_map/all_to_all | solution.py:109
  76.2 0.6 gather_fusion.1
  77.0 2.0 %fusion.38 = f32[4,1024]{1,0:T(4,128)S(1)} fusion(bf16[4,1024]{1,0:T(4,128)(2,1)S(1)} %add_convert_fusion, bf16[1024,1024]{1,0:T(8,128)(2,1)} %param.20), kind=kOutput, calls=%fused_computation.81 | convolution fusion | flops 8388608 | bytes 2121728 | tf_op jit(solution)/shard_map/dot_general | solution.py:102
  79.0 10.3 %all-reduce = bf16[4,1024]{1,0:T(4,128)(2,1)S(1)} all-reduce(f32[4,1024]{1,0:T(4,128)S(1)} %fusion.38), channel_id=2, replica_groups=mesh['groups'=2,'ep'=4,'tp'=4] {'tp'}, use_global_device_ids=true, to_apply=%region_8.9.clone | all-reduce | flops 4096 | bytes 24576
  89.2 0.7 fusion.18
  90.4 3.4 %all-to-all-start.3 = ((bf16[4,80,256]{2,1,0:T(8,128)(2,1)}), bf16[4,80,256]{2,1,0:T(8,128)(2,1)S(1)}, u32[]{:S(2)}, u32[]{:S(2)}) async-start(bf16[4,80,256]{2,1,0:T(8,128)(2,1)} %all-to-all-done.2), calls=%async_computation.3 | async-start | bytes 327680 | tf_op jit(solution)/shard_map/all_to_all | solution.py:108
  93.8 4.9 %all-to-all-done.3 = bf16[4,80,256]{2,1,0:T(8,128)(2,1)S(1)} async-done(((bf16[4,80,256]{2,1,0:T(8,128)(2,1)}), bf16[4,80,256]{2,1,0:T(8,128)(2,1)S(1)}, u32[]{:S(2)}, u32[]{:S(2)}) %all-to-all-start.3) | async-done | bytes 163872 | tf_op jit(solution)/shard_map/all_to_all | solution.py:108
  98.8 0.2 fusion.36
  99.0 0.2 fusion.37
  99.3 0.2 fusion.13
  99.5 0.2 fusion.11
  99.7 0.6 convert_element_type.95
  (47 shorter events, 1.5 us)
Async XLA Ops:
  7.2 16.3 %copy-start = (bf16[1,1024,1024]{2,1,0:T(8,128)(2,1)S(1)}, bf16[1,1024,1024]{2,1,0:T(8,128)(2,1)}, u32[]{:S(2)}) copy-start(bf16[1,1024,1024]{2,1,0:T(8,128)(2,1)} %param.18) | copy-start | bytes 6291460
  11.5 12.0 %all-to-all-start = ((bf16[4,3,1024]{2,1,0:T(4,128)(2,1)}), bf16[4,3,1024]{2,1,0:T(4,128)(2,1)S(1)}, u32[]{:S(2)}, u32[]{:S(2)}) async-start(bf16[4,3,1024]{2,1,0:T(4,128)(2,1)} %copy.36), calls=%async_computation | async-start | bytes 65536 | tf_op jit(solution)/shard_map/all_to_all | solution.py:87
  17.8 41.4 %all-reduce.4.cloned.1.call-start = ((), (), s32[]{:S(2)}) async-start(), calls=%async_computation.4 | async-start | bytes 262144 | tf_op jit(solution)/shard_map/psum | solution.py:92
  23.5 1.6 %copy-start.1 = (bf16[1,1024,1024]{2,1,0:T(8,128)(2,1)S(1)}, bf16[1,1024,1024]{2,1,0:T(8,128)(2,1)}, u32[]{:S(2)}) copy-start(bf16[1,1024,1024]{2,1,0:T(8,128)(2,1)} %param.17) | copy-start | bytes 6291460
  25.1 41.5 %copy-start.3 = (bf16[1,8192]{1,0:T(2,128)(2,1)S(1)}, bf16[1,8192]{1,0:T(2,128)(2,1)}, u32[]{:S(2)}) copy-start(bf16[1,8192]{1,0:T(2,128)(2,1)} %param.25) | copy-start | bytes 49156
  25.1 41.6 %copy-start.6 = (u32[32]{0:T(128)S(1)}, u32[32]{0:T(128)}, u32[]{:S(2)}) copy-start(u32[32]{0:T(128)} %constant.104) | copy-start | bytes 388
  26.1 50.8 %copy-start.4 = (bf16[4,1024]{1,0:T(4,128)(2,1)S(1)}, bf16[4,1024]{1,0:T(4,128)(2,1)}, u32[]{:S(2)}) copy-start(bf16[4,1024]{1,0:T(4,128)(2,1)} %param.14) | copy-start | bytes 24580
  59.2 30.9 %copy-start.5 = (f32[128]{0:T(128)S(1)}, f32[128]{0:T(128)}, u32[]{:S(2)}) copy-start(f32[128]{0:T(128)} %param.21) | copy-start | bytes 1540
  61.9 10.3 %all-to-all-start.1 = ((bf16[4,3,1024]{2,1,0:T(4,128)(2,1)}), bf16[4,3,1024]{2,1,0:T(4,128)(2,1)S(1)}, u32[]{:S(2)}, u32[]{:S(2)}) async-start(bf16[4,3,1024]{2,1,0:T(4,128)(2,1)} %reshape.354), calls=%async_computation.1 | async-start | bytes 65536 | tf_op jit(solution)/shard_map/all_to_all | solution.py:96
  72.2 18.3 %all-to-all-start.2 = ((bf16[4,80,256]{2,1,0:T(8,128)(2,1)}), bf16[4,80,256]{2,1,0:T(8,128)(2,1)}, u32[]{:S(2)}, u32[]{:S(2)}) async-start(bf16[4,80,256]{2,1,0:T(8,128)(2,1)} %broadcast_select_fusion), calls=%async_computation.2 | async-start | bytes 327680 | tf_op jit(solution)/shard_map/all_to_all | solution.py:109
  77.0 23.4 %copy-start.2 = (bf16[4,1024]{1,0:T(4,128)(2,1)}, bf16[4,1024]{1,0:T(4,128)(2,1)S(1)}, u32[]{:S(2)}) copy-start(bf16[4,1024]{1,0:T(4,128)(2,1)S(1)} %add_convert_fusion) | copy-start | bytes 24580
  90.4 8.3 %all-to-all-start.3 = ((bf16[4,80,256]{2,1,0:T(8,128)(2,1)}), bf16[4,80,256]{2,1,0:T(8,128)(2,1)S(1)}, u32[]{:S(2)}, u32[]{:S(2)}) async-start(bf16[4,80,256]{2,1,0:T(8,128)(2,1)} %all-to-all-done.2), calls=%async_computation.3 | async-start | bytes 327680 | tf_op jit(solution)/shard_map/all_to_all | solution.py:108
Sparse Core Ops, SparseCore 0:
  26.3 32.8 all-reduce.3
where the time goes:
time: 108 us; the launch traced here: 107 us
  waiting for transfers between devices  42.8 us (40%)
  starting transfers between devices  18.2 us (17%)
  between operations  14.9 us (14%)
  blocking collectives  10.3 us (10%)
  local copies, waits for them, and re-layouts  9.84 us (9%)
  matrix products  6.64 us (6%)
  other arithmetic  4.52 us (4%)
    psum x1, waiting for transfers between devices, on_device(): gate, up = lax.psum((gate, up), 'tp')  33 us
    unnamed x1, blocking collectives  10.3 us
    all_to_all x1, starting transfers between devices, on_device(): lax.all_to_all(outgoing, 'ep', split_axis=0, concat_axis=0, tiled=True)  6.32 us
    all_to_all x1, waiting for transfers between devices, on_device(): lax.all_to_all(lax.all_to_all(arranged, 'ep', split_axis=0, concat_axis=0...  4.94 us
    all_to_all x1, waiting for transfers between devices, on_device(): lax.all_to_all(result, 'ep', split_axis=0, concat_axis=0, tiled=True)  4.79 us
    all_to_all x1, starting transfers between devices, on_device(): lax.all_to_all(result, 'ep', split_axis=0, concat_axis=0, tiled=True)  4.6 us
    all_to_all x1, starting transfers between devices, on_device(): lax.all_to_all(arranged, 'ep', split_axis=0, concat_axis=0, tiled=True)  3.97 us
    all_to_all x1, starting transfers between devices, on_device(): lax.all_to_all(lax.all_to_all(arranged, 'ep', split_axis=0, concat_axis=0...  3.35 us
  transfers between devices with their start and end apart: 5, of which 4 were waited for; matrix products, arithmetic and copies ran while one was open for 9% of the time, Pallas kernels for 0%

commit v1 on v0

v1 whole, which is shorter than its diff:
```python
import functools
import math

import jax
import jax.numpy as jnp
from jax import lax
from jax.experimental import pallas as pl
from jax.experimental.pallas import tpu as pltpu
from jax.sharding import PartitionSpec as P

KVH = 4
HD = 128
MESH = pl.DeviceIdType.MESH
F32 = jnp.float32
BF16 = jnp.bfloat16


def flip(index, mask):
    out = index
    bit = 1
    while bit <= mask:
        if mask & bit:
            out = out + bit - 2 * bit * ((index // bit) % 2)
        bit *= 2
    return out


def kernel(
    N, T, R, M, PJ, CTX, KF, FS,
    x_hbm, res_hbm, ids_ref, rw_ref, wg_hbm, wu_hbm, wd_hbm, wkv_hbm, gain_ref,
    kv_hbm, order_ref, len_ref, q_hbm,
    hid_ref, att_ref,
    xbuf, xs, wg_v, wu_v, wd_v, wkv_v, res_v, q_v, qs, kv_v, abuf, cbuf,
    sbuf, rbuf, ibuf, rs, obuf, ebuf, fs, fbuf, frecv,
    lsem, wsem, xs_s, xs_r, c_s, c_r, g_s, g_r, i_s, i_r, e_s, e_r, f_s, f_r,
):
    group = lax.axis_index("groups")
    me = lax.axis_index("ep")
    mt = lax.axis_index("tp")
    QG = qs.shape[1] // KVH

    def dev(e, t):
        return (group, e, t)

    def remote(src, dst, ssem, rsem, e, t):
        return pltpu.make_async_remote_copy(
            src_ref=src, dst_ref=dst, send_sem=ssem, recv_sem=rsem,
            device_id=dev(e, t), device_id_type=MESH,
        )

    peers = [flip(mt, T - 1 - k) for k in range(T)]
    nexts = [lax.rem(me + j, N) for j in range(N)]

    load_kv = pltpu.make_async_copy(kv_hbm.at[0], kv_v, lsem.at[0])
    load_kv.start()
    load_x = pltpu.make_async_copy(x_hbm, xbuf.at[0], lsem.at[1])
    load_x.start()
    load_w = []
    for k in range(T):
        cols = pl.ds(pl.multiple_of(peers[k] * FS, FS), FS)
        a = pltpu.make_async_copy(wg_hbm.at[0, :, cols], wg_v.at[k], wsem.at[0, k])
        b = pltpu.make_async_copy(wu_hbm.at[0, :, cols], wu_v.at[k], wsem.at[1, k])
        a.start()
        b.start()
        load_w.append((a, b))
    load_q = pltpu.make_async_copy(q_hbm, q_v, lsem.at[2])
    load_q.start()
    load_d = pltpu.make_async_copy(wd_hbm.at[0], wd_v, lsem.at[3])
    load_d.start()
    load_r = pltpu.make_async_copy(res_hbm, res_v, lsem.at[4])
    load_r.start()
    load_k = pltpu.make_async_copy(wkv_hbm, wkv_v, lsem.at[5])
    load_k.start()

    barrier = pltpu.get_barrier_semaphore()
    for j in range(1, N):
        pl.semaphore_signal(barrier, inc=1, device_id=dev(nexts[j], mt), device_id_type=MESH)
    for k in range(T - 1):
        pl.semaphore_signal(barrier, inc=1, device_id=dev(me, peers[k]), device_id_type=MESH)
    expected = N - 1 + T - 1
    for m in range(M):
        p = (mt * M + m) // PJ
        for t in range(T):
            @pl.when(jnp.logical_not((p == me) & (mt == t)))
            def _():
                pl.semaphore_signal(barrier, inc=1, device_id=dev(p, t), device_id_type=MESH)
    for j in range(PJ):
        expected = expected + N - jnp.where((me * PJ + j) // M == mt, 1, 0)

    load_kv.wait()
    for i in range(N * PJ):
        abuf[i] = kv_v[order_ref[0, i]]
    load_x.wait()
    pl.semaphore_wait(barrier, expected)

    dispatch = []
    for j in range(1, N):
        c = remote(xbuf.at[0], xbuf.at[j], xs_s.at[j], xs_r.at[j], nexts[j], mt)
        c.start()
        dispatch.append(c)

    def cache_copy(d, j):
        place = me * PJ + j
        t = place // M
        m = place % M
        i = d * PJ + j
        return (d == me) & (t == mt), m, remote(
            abuf.at[i], cbuf.at[mt, m], c_s.at[i], c_r.at[mt, m], d, t
        )

    for d in range(N):
        for j in range(PJ):
            own, m, c = cache_copy(d, j)

            @pl.when(own)
            def _():
                cbuf[mt, m] = abuf[d * PJ + j]

            @pl.when(jnp.logical_not(own))
            def _():
                c.start()

    load_q.wait()
    for m in range(M):
        for h in range(qs.shape[1]):
            qs[m, h : h + 1, :] = q_v[m : m + 1, h * HD : (h + 1) * HD].astype(F32)
    lane = lax.broadcasted_iota(jnp.int32, (1, HD), 1)
    half = jnp.where(lane < HD // 2, lane, lane - HD // 2).astype(F32)
    frequency = jnp.exp(half * F32(-2.0 / HD * math.log(1000000.0)))
    turns = []
    for m in range(M):
        angle = len_ref[m].astype(F32) * frequency
        sine = jnp.sin(angle)
        turns.append((jnp.cos(angle), jnp.where(lane < HD // 2, -sine, sine)))

    for c in dispatch:
        c.wait_recv()
    for e in range(N):
        slot = lax.rem(me - e + N, N)
        xs[e * R : (e + 1) * R, :] = xbuf[slot].astype(F32)
    x = xs[...].astype(BF16)

    scatter = []
    for k in range(T):
        load_w[k][0].wait()
        gate = jnp.dot(x, wg_v[k], preferred_element_type=F32)
        load_w[k][1].wait()
        up = jnp.dot(x, wu_v[k], preferred_element_type=F32)
        if k < T - 1:
            sbuf[k, :, :FS] = gate.astype(BF16)
            sbuf[k, :, FS:] = up.astype(BF16)
            c = remote(sbuf.at[k], rbuf.at[k], g_s.at[k], g_r.at[k], me, peers[k])
            c.start()
            scatter.append(c)
    for k in range(T - 2, -1, -1):
        scatter[k].wait_recv()
        gate = gate + rbuf[k, :, :FS].astype(F32)
        up = up + rbuf[k, :, FS:].astype(F32)
    ibuf[T - 1] = (gate / (1.0 + jnp.exp(-gate)) * up).astype(BF16)
    gather = []
    for k in range(T - 1):
        c = remote(ibuf.at[T - 1], ibuf.at[k], i_s.at[k], i_r.at[k], me, peers[k])
        c.start()
        gather.append(c)

    load_d.wait()

    def down(k):
        rows = pl.ds(pl.multiple_of(peers[k] * FS, FS), FS)
        return jnp.dot(ibuf[k], wd_v[rows, :], preferred_element_type=F32)

    total = down(T - 1)
    for k in range(T - 2, -1, -1):
        gather[k].wait_recv()
        total = total + down(k)
    rs[...] = total
    for d in range(N):
        obuf[d] = rs[d * R : (d + 1) * R, :].astype(BF16)
    back = []
    for j in range(1, N):
        c = remote(obuf.at[nexts[j]], ebuf.at[j], e_s.at[j], e_r.at[j], nexts[j], mt)
        c.start()
        back.append(c)

    scale = F32(1.0 / math.sqrt(HD))
    parts = []
    for m in range(M):
        p = (mt * M + m) // PJ
        for t in range(T):
            @pl.when(jnp.logical_not((p == me) & (mt == t)))
            def _():
                remote(abuf.at[0], cbuf.at[t, m], c_s.at[0], c_r.at[t, m], p, t).wait_recv()
        live = lax.broadcasted_iota(jnp.int32, (QG, CTX), 1) < len_ref[m]
        for g in range(KVH):
            at = g * 2 * HD
            keys = cbuf[at // KF, m, :, at % KF : at % KF + HD]
            at = at + HD
            values = cbuf[at // KF, m, :, at % KF : at % KF + HD]
            query = qs[m, g * QG : (g + 1) * QG, :]
            scores = lax.dot_general(
                query.astype(BF16), keys, (((1,), (1,)), ((), ())), preferred_element_type=F32
            ) * scale
            scores = jnp.where(live, scores, F32(-1e30))
            top = jnp.max(scores, axis=1, keepdims=True)
            weights = jnp.where(live, jnp.exp(scores - top), F32(0.0))
            parts.append((
                query, top, jnp.sum(weights, axis=1, keepdims=True),
                jnp.dot(weights.astype(BF16), values, preferred_element_type=F32),
            ))

    share = rw_ref[...] / jnp.sum(rw_ref[...], axis=1, keepdims=True)
    load_r.wait()
    mixed = res_v[...].astype(F32)
    for j in range(N):
        if j:
            back[j - 1].wait_recv()
        e = lax.rem(me - j + N, N)
        weight = jnp.sum(jnp.where(ids_ref[...] == e, share, F32(0.0)), axis=1, keepdims=True)
        block = ebuf[j] if j else obuf[me]
        mixed = mixed + weight * block.astype(F32)
    hidden = mixed.astype(BF16)
    hid_ref[...] = hidden
    load_k.wait()
    fs[...] = jnp.dot(hidden, wkv_v[...], preferred_element_type=F32)
    for t in range(T):
        fbuf[t] = fs[t * M : (t + 1) * M, :]
    sums = []
    for k in range(T - 1):
        c = remote(fbuf.at[peers[k]], frecv.at[k], f_s.at[k], f_r.at[k], me, peers[k])
        c.start()
        sums.append(c)
    fresh = fbuf[mt]
    for k in range(T - 2, -1, -1):
        sums[k].wait_recv()
        fresh = fresh + frecv[k]
    fresh = fresh.astype(BF16).astype(F32)

    for m in range(M):
        cosine, sine = turns[m]
        for g in range(KVH):
            at = g * 2 * HD
            key = fresh[m : m + 1, at : at + HD]
            value = fresh[m : m + 1, at + HD : at + 2 * HD]
            factor = lax.rsqrt(jnp.mean(key * key, axis=1, keepdims=True) + F32(1e-6))
            key = key * factor * gain_ref[...]
            key = (key * cosine + pltpu.roll(key, HD // 2, 1) * sine).astype(BF16).astype(F32)
            query, top, weight, summed = parts[m * KVH + g]
            score = jnp.sum(query * key, axis=1, keepdims=True) * scale
            most = jnp.maximum(top, score)
            old = jnp.exp(top - most)
            new = jnp.exp(score - most)
            out = (summed * old + new * value) / (weight * old + new)
            att_ref[m, g * QG : (g + 1) * QG, :] = out.astype(BF16)

    for c in dispatch + scatter + gather + back + sums:
        c.wait_send()
    for d in range(N):
        for j in range(PJ):
            own, m, c = cache_copy(d, j)

            @pl.when(jnp.logical_not(own))
            def _():
                c.wait_send()


def on_device(
    normed, residual, expert_ids, route_weight, w_gate, w_up, w_down, w_kv,
    key_gain, prefill_kv, order, lengths, queries,
):
    N = lax.axis_size("ep")
    T = lax.axis_size("tp")
    R, W = normed.shape
    M = lengths.shape[0]
    _, requests, CTX, KF = prefill_kv.shape
    PJ = requests // N
    FF = w_gate.shape[2]
    FS = FF // T
    KVF = w_kv.shape[1]
    heads = queries.shape[1] // HD
    rows = N * R
    dma = pltpu.SemaphoreType.DMA
    anywhere = pl.BlockSpec(memory_space=pl.ANY)
    vmem = pl.BlockSpec(memory_space=pltpu.VMEM)
    smem = pl.BlockSpec(memory_space=pltpu.SMEM)
    hidden_state, attention = pl.pallas_call(
        functools.partial(kernel, N, T, R, M, PJ, CTX, KF, FS),
        out_shape=(
            jax.ShapeDtypeStruct((R, W), BF16),
            jax.ShapeDtypeStruct((M, heads, HD), BF16),
        ),
        in_specs=[
            anywhere, anywhere, vmem, vmem, anywhere, anywhere, anywhere, anywhere, vmem,
            anywhere, smem, smem, anywhere,
        ],
        out_specs=(vmem, vmem),
        scratch_shapes=[
            pltpu.VMEM((N, R, W), BF16),
            pltpu.VMEM((rows, W), F32),
            pltpu.VMEM((T, W, FS), BF16),
            pltpu.VMEM((T, W, FS), BF16),
            pltpu.VMEM((FF, W), BF16),
            pltpu.VMEM((W, KVF), BF16),
            pltpu.VMEM((R, W), BF16),
            pltpu.VMEM((M, heads * HD), BF16),
            pltpu.VMEM((M, heads, HD), F32),
            pltpu.VMEM((requests, CTX, KF), BF16),
            pltpu.VMEM((requests, CTX, KF), BF16),
            pltpu.VMEM((T, M, CTX, KF), BF16),
            pltpu.VMEM((T - 1, rows, 2 * FS), BF16),
            pltpu.VMEM((T - 1, rows, 2 * FS), BF16),
            pltpu.VMEM((T, rows, FS), BF16),
            pltpu.VMEM((rows, W), F32),
            pltpu.VMEM((N, R, W), BF16),
            pltpu.VMEM((N, R, W), BF16),
            pltpu.VMEM((R, KVF), F32),
            pltpu.VMEM((T, M, KVF), F32),
            pltpu.VMEM((T - 1, M, KVF), F32),
            dma((6,)), dma((2, T)),
            dma((N,)), dma((N,)),
            dma((requests,)), dma((T, M)),
            dma((T - 1,)), dma((T - 1,)),
            dma((T - 1,)), dma((T - 1,)),
            dma((N,)), dma((N,)),
            dma((T - 1,)), dma((T - 1,)),
        ],
        compiler_params=pltpu.CompilerParams(
            collective_id=0, has_side_effects=True, vmem_limit_bytes=48 * 1024 * 1024
        ),
    )(
        normed, residual, expert_ids, route_weight, w_gate, w_up, w_down, w_kv,
        key_gain.reshape(1, HD), prefill_kv, order, lengths, queries,
    )
    return hidden_state, attention.reshape(M, heads * HD)


def solution(mesh):
    in_specs = (
        P(("groups", "ep"), "tp"),
        P(("groups", "ep"), "tp"),
        P(("groups", "ep"), None),
        P(("groups", "ep"), None),
        P("ep", "tp", None),
        P("ep", "tp", None),
        P("ep", None, "tp"),
        P("tp", None),
        P(),
        P(("groups", "ep"), None, None, "tp"),
        P(("groups", "ep"), None),
        P(("groups", "ep", "tp")),
        P(("groups", "ep", "tp"), None),
    )
    out_specs = (P(("groups", "ep"), "tp"), P(("groups", "ep", "tp"), None))
    return jax.shard_map(
        on_device, mesh=mesh, in_specs=in_specs, out_specs=out_specs, check_vma=False
    )
```

time: 108 us -> 37.3 us (0.35)
  waiting for transfers between devices: 42.8 us -> 0 us
  Pallas kernels: 0 us -> 25.3 us
  starting transfers between devices: 18.2 us -> 0 us
  between operations: 14.9 us -> 1.29 us
  blocking collectives: 10.3 us -> 0 us
  matrix products: 6.64 us -> 0 us
  other arithmetic: 4.52 us -> 0 us
    psum x1 -> x0, waiting for transfers between devices: 33 us -> none  [on_device(): gate, up = lax.psum((gate, up), 'tp')]
    pallas_call x0 -> x1, Pallas kernels: none -> 25.3 us  [on_device(): pl.pallas_call(functools.partial(kernel, N, T, R, M, PJ, CTX, KF, FS), ou...]
    all_to_all x4 -> x0, starting transfers between devices: 18.2 us -> none  [the longest x1 6.32 us: on_device(): lax.all_to_all(outgoing, 'ep', split_axis=0, concat_axis=0, tiled=True)]
    unnamed x1 -> x0, blocking collectives: 10.3 us -> none
    all_to_all x4 -> x0, waiting for transfers between devices: 9.8 us -> none  [the longest x1 4.94 us: on_device(): lax.all_to_all(lax.all_to_all(arranged, 'ep', split_axis=0, concat_axis=0...]
    unnamed x16 -> x20, local copies, waits for them, and re-layouts: 2.2 us -> 10.3 us
    dot_general x7 -> x0, matrix products: 6.64 us -> none  [the longest x1 2.06 us: on_device(): jnp.dot(inner, w_down[0], preferred_element_type=jnp.float32)]
    gather x3 -> x0, local copies, waits for them, and re-layouts: 3.38 us -> none  [the longest x1 1.47 us: on_device(): arranged = jnp.take(prefill_kv[0], order[0], axis=0)]
  transfers between devices with their start and end apart: 5 -> 0, of which waited for: 4 -> 0; matrix products, arithmetic and copies ran while one was open for 9% -> 0% of each run, Pallas kernels for 0% -> 0%
where the time goes in v1:
time: 37.3 us; the launch traced here: 36.9 us
  Pallas kernels  25.3 us (68%)
  local copies, waits for them, and re-layouts  10.3 us (28%)
  between operations  1.29 us (3%)
    pallas_call x1, Pallas kernels, on_device(): pl.pallas_call(functools.partial(kernel, N, T, R, M, PJ, CTX, KF, FS), ou...  25.3 us
    unnamed x20, local copies, waits for them, and re-layouts  10.3 us

profile of v1, /device:TPU:0, one launch (start us, length us, event | category | flops | bytes accessed | tf_op | source)
XLA Modules:
  0.0 36.9 jit_solution(4761990243248801164)
XLA Ops:
  1.3 0.8 %copy.15.ids_ref = s32[4,2]{1,0:T(4,128)S(1)} copy(s32[4,2]{0,1:T(2,128)} %param.15) | data formatting | bytes 64 | tf_op args[2]
  2.0 0.8 %copy.16.rw_ref = f32[4,2]{1,0:T(4,128)S(1)} copy(f32[4,2]{0,1:T(2,128)} %param.16) | data formatting | bytes 64 | tf_op args[3]
  2.8 0.0 copy-start
  2.8 1.6 %copy-done = bf16[1,1024,1024]{2,1,0:T(8,128)(2,1)S(1)} copy-done((bf16[1,1024,1024]{2,1,0:T(8,128)(2,1)S(1)}, bf16[1,1024,1024]{2,1,0:T(8,128)(2,1)}, u32[]{:S(2)}) %copy-start) | copy-done | bytes 2097176
  4.4 0.0 copy-start.1
  4.4 1.6 %copy-done.1 = bf16[1,1024,1024]{2,1,0:T(8,128)(2,1)S(1)} copy-done((bf16[1,1024,1024]{2,1,0:T(8,128)(2,1)S(1)}, bf16[1,1024,1024]{2,1,0:T(8,128)(2,1)}, u32[]{:S(2)}) %copy-start.1) | copy-done | bytes 2097176
  6.0 0.0 copy-start.2
  6.0 0.9 %copy-done.2 = bf16[1,4,80,256]{3,2,1,0:T(8,128)(2,1)S(1)} copy-done((bf16[1,4,80,256]{3,2,1,0:T(8,128)(2,1)S(1)}, bf16[1,4,80,256]{3,2,1,0:T(8,128)(2,1)}, u32[]{:S(2)}) %copy-start.2) | copy-done | bytes 163864
  6.9 0.0 copy-start.3
  6.9 0.8 %copy-done.3 = bf16[1,8192]{1,0:T(2,128)(2,1)S(1)} copy-done((bf16[1,8192]{1,0:T(2,128)(2,1)S(1)}, bf16[1,8192]{1,0:T(2,128)(2,1)}, u32[]{:S(2)}) %copy-start.3) | copy-done | bytes 16408
  7.7 0.0 copy-start.4
  7.7 0.7 %copy-done.4 = bf16[4,1024]{1,0:T(4,128)(2,1)S(1)} copy-done((bf16[4,1024]{1,0:T(4,128)(2,1)S(1)}, bf16[4,1024]{1,0:T(4,128)(2,1)}, u32[]{:S(2)}) %copy-start.4) | copy-done | bytes 8216
  8.4 0.0 copy-start.5
  8.4 0.7 %copy-done.5 = bf16[4,1024]{1,0:T(4,128)(2,1)S(1)} copy-done((bf16[4,1024]{1,0:T(4,128)(2,1)S(1)}, bf16[4,1024]{1,0:T(4,128)(2,1)}, u32[]{:S(2)}) %copy-start.5) | copy-done | bytes 8216
  9.1 0.0 copy-start.6
  9.1 0.7 %copy-done.6 = f32[128]{0:T(128)S(1)} copy-done((f32[128]{0:T(128)S(1)}, f32[128]{0:T(128)}, u32[]{:S(2)}) %copy-start.6) | copy-done | bytes 536
  9.7 0.0 copy-start.7
  9.7 0.7 %copy-done.7 = s32[1,4]{1,0:T(1,128)S(1)} copy-done((s32[1,4]{1,0:T(1,128)S(1)}, s32[1,4]{1,0:T(1,128)}, u32[]{:S(2)}) %copy-start.7) | copy-done | bytes 40
  10.4 25.3 %shard_map.140 = (bf16[4,1024]{1,0:T(4,128)(2,1)S(1)}, bf16[1,64,128]{2,1,0:T(8,128)(2,1)S(1)}) custom-call(bf16[4,1024]{1,0:T(4,128)(2,1)S(1)} %copy-done.4, bf16[4,1024]{1,0:T(4,128)(2,1)S(1)} %copy-done.5, s32[4,2]{1,0:T(4,128)S(1)} %copy.15.ids_ref, f32[4,2]{1,0:T(4,128)S(1)} %copy.16.rw_ref, bf16[1,1024,1024]{2,1,0:T(8,128)(2,1)S(1)} %copy-done, ...), custom_call_target="tpu_custom_call" | custom-call | tf_op jit(solution)/shard_map/pallas_call | solution.py:285
  35.6 0.6 %copy.19 = bf16[1,1,64,128]{3,1,2,0:T(2,128)(2,1)} copy(bf16[1,1,64,128]{3,2,1,0:T(8,128)(2,1)S(1)} %bitcast.5) | data formatting | bytes 32768
  36.3 0.6 %copy.22 = bf16[4,1024]{1,0:T(4,128)(2,1)} copy(bf16[4,1024]{1,0:T(4,128)(2,1)S(1)} %get-tuple-element.8) | data formatting | bytes 16384
Async XLA Ops:
  2.8 1.6 %copy-start = (bf16[1,1024,1024]{2,1,0:T(8,128)(2,1)S(1)}, bf16[1,1024,1024]{2,1,0:T(8,128)(2,1)}, u32[]{:S(2)}) copy-start(bf16[1,1024,1024]{2,1,0:T(8,128)(2,1)} %wg_hbm.1) | copy-start | bytes 6291460
  4.4 1.6 %copy-start.1 = (bf16[1,1024,1024]{2,1,0:T(8,128)(2,1)S(1)}, bf16[1,1024,1024]{2,1,0:T(8,128)(2,1)}, u32[]{:S(2)}) copy-start(bf16[1,1024,1024]{2,1,0:T(8,128)(2,1)} %wu_hbm.1) | copy-start | bytes 6291460
  6.0 0.9 %copy-start.2 = (bf16[1,4,80,256]{3,2,1,0:T(8,128)(2,1)S(1)}, bf16[1,4,80,256]{3,2,1,0:T(8,128)(2,1)}, u32[]{:S(2)}) copy-start(bf16[1,4,80,256]{3,2,1,0:T(8,128)(2,1)} %kv_hbm.1) | copy-start | bytes 491524
  6.9 0.8 %copy-start.3 = (bf16[1,8192]{1,0:T(2,128)(2,1)S(1)}, bf16[1,8192]{1,0:T(2,128)(2,1)}, u32[]{:S(2)}) copy-start(bf16[1,8192]{1,0:T(2,128)(2,1)} %q_hbm.1) | copy-start | bytes 49156
  7.7 0.7 %copy-start.4 = (bf16[4,1024]{1,0:T(4,128)(2,1)S(1)}, bf16[4,1024]{1,0:T(4,128)(2,1)}, u32[]{:S(2)}) copy-start(bf16[4,1024]{1,0:T(4,128)(2,1)} %x_hbm.1) | copy-start | bytes 24580
  8.4 0.7 %copy-start.5 = (bf16[4,1024]{1,0:T(4,128)(2,1)S(1)}, bf16[4,1024]{1,0:T(4,128)(2,1)}, u32[]{:S(2)}) copy-start(bf16[4,1024]{1,0:T(4,128)(2,1)} %res_hbm.1) | copy-start | bytes 24580
  9.1 0.7 %copy-start.6 = (f32[128]{0:T(128)S(1)}, f32[128]{0:T(128)}, u32[]{:S(2)}) copy-start(f32[128]{0:T(128)} %param.21) | copy-start | bytes 1540
  9.7 0.7 %copy-start.7 = (s32[1,4]{1,0:T(1,128)S(1)}, s32[1,4]{1,0:T(1,128)}, u32[]{:S(2)}) copy-start(s32[1,4]{1,0:T(1,128)} %order_ref.1) | copy-start | bytes 52

commit v2 on v1

--- a/solution.py
+++ b/solution.py
@@ -27,9 +27,10 @@
 
 def kernel(
     N, T, R, M, PJ, CTX, KF, FS,
-    x_hbm, res_hbm, ids_ref, rw_ref, wg_hbm, wu_hbm, wd_hbm, wkv_hbm, gain_ref,
-    kv_hbm, order_ref, len_ref, q_hbm,
+    x_hbm, res_hbm, ids_hbm, rw_hbm, wg_hbm, wu_hbm, wd_hbm, wkv_hbm, gain_hbm,
+    kv_hbm, order_hbm, len_hbm, q_hbm,
     hid_ref, att_ref,
+    ids_ref, rw_ref, gain_ref, order_ref, len_ref,
     xbuf, xs, wg_v, wu_v, wd_v, wkv_v, res_v, q_v, qs, kv_v, abuf, cbuf,
     sbuf, rbuf, ibuf, rs, obuf, ebuf, fs, fbuf, frecv,
     lsem, wsem, xs_s, xs_r, c_s, c_r, g_s, g_r, i_s, i_r, e_s, e_r, f_s, f_r,
@@ -51,10 +52,20 @@
     peers = [flip(mt, T - 1 - k) for k in range(T)]
     nexts = [lax.rem(me + j, N) for j in range(N)]
 
+    load_x = pltpu.make_async_copy(x_hbm, xbuf.at[0], lsem.at[1])
+    load_x.start()
+    load_o = pltpu.make_async_copy(order_hbm, order_ref, lsem.at[6])
+    load_o.start()
     load_kv = pltpu.make_async_copy(kv_hbm.at[0], kv_v, lsem.at[0])
     load_kv.start()
-    load_x = pltpu.make_async_copy(x_hbm, xbuf.at[0], lsem.at[1])
-    load_x.start()
+    load_l = pltpu.make_async_copy(len_hbm, len_ref, lsem.at[7])
+    load_l.start()
+    load_i = pltpu.make_async_copy(ids_hbm, ids_ref, lsem.at[8])
+    load_i.start()
+    load_s = pltpu.make_async_copy(rw_hbm, rw_ref, lsem.at[9])
+    load_s.start()
+    load_g = pltpu.make_async_copy(gain_hbm, gain_ref, lsem.at[10])
+    load_g.start()
     load_w = []
     for k in range(T):
         cols = pl.ds(pl.multiple_of(peers[k] * FS, FS), FS)
@@ -87,9 +98,6 @@
     for j in range(PJ):
         expected = expected + N - jnp.where((me * PJ + j) // M == mt, 1, 0)
 
-    load_kv.wait()
-    for i in range(N * PJ):
-        abuf[i] = kv_v[order_ref[0, i]]
     load_x.wait()
     pl.semaphore_wait(barrier, expected)
 
@@ -108,8 +116,11 @@
             abuf.at[i], cbuf.at[mt, m], c_s.at[i], c_r.at[mt, m], d, t
         )
 
+    load_o.wait()
+    load_kv.wait()
     for d in range(N):
         for j in range(PJ):
+            abuf[d * PJ + j] = kv_v[order_ref[0, d * PJ + j]]
             own, m, c = cache_copy(d, j)
 
             @pl.when(own)
@@ -121,6 +132,8 @@
                 c.start()
 
     load_q.wait()
+    load_l.wait()
+    load_g.wait()
     for m in range(M):
         for h in range(qs.shape[1]):
             qs[m, h : h + 1, :] = q_v[m : m + 1, h * HD : (h + 1) * HD].astype(F32)
@@ -208,16 +221,25 @@
                 jnp.dot(weights.astype(BF16), values, preferred_element_type=F32),
             ))
 
-    share = rw_ref[...] / jnp.sum(rw_ref[...], axis=1, keepdims=True)
+    load_i.wait()
+    load_s.wait()
+    share = rw_ref[...] / jnp.sum(rw_ref[...], axis=0, keepdims=True)
+    diagonal = lax.broadcasted_iota(jnp.int32, (R, R), 0) == lax.broadcasted_iota(
+        jnp.int32, (R, R), 1
+    )
+
+    def weight_of(e):
+        row = jnp.sum(jnp.where(ids_ref[...] == e, share, F32(0.0)), axis=0, keepdims=True)
+        return jnp.sum(jnp.where(diagonal, row, F32(0.0)), axis=1, keepdims=True)
+
     load_r.wait()
     mixed = res_v[...].astype(F32)
     for j in range(N):
         if j:
             back[j - 1].wait_recv()
         e = lax.rem(me - j + N, N)
-        weight = jnp.sum(jnp.where(ids_ref[...] == e, share, F32(0.0)), axis=1, keepdims=True)
         block = ebuf[j] if j else obuf[me]
-        mixed = mixed + weight * block.astype(F32)
+        mixed = mixed + weight_of(e) * block.astype(F32)
     hidden = mixed.astype(BF16)
     hid_ref[...] = hidden
     load_k.wait()
@@ -278,22 +300,24 @@
     KVF = w_kv.shape[1]
     heads = queries.shape[1] // HD
     rows = N * R
+    choices = expert_ids.shape[1]
     dma = pltpu.SemaphoreType.DMA
-    anywhere = pl.BlockSpec(memory_space=pl.ANY)
+    hbm = pl.BlockSpec(memory_space=pltpu.HBM)
     vmem = pl.BlockSpec(memory_space=pltpu.VMEM)
-    smem = pl.BlockSpec(memory_space=pltpu.SMEM)
     hidden_state, attention = pl.pallas_call(
         functools.partial(kernel, N, T, R, M, PJ, CTX, KF, FS),
         out_shape=(
             jax.ShapeDtypeStruct((R, W), BF16),
             jax.ShapeDtypeStruct((M, heads, HD), BF16),
         ),
-        in_specs=[
-            anywhere, anywhere, vmem, vmem, anywhere, anywhere, anywhere, anywhere, vmem,
-            anywhere, smem, smem, anywhere,
-        ],
+        in_specs=[hbm] * 13,
         out_specs=(vmem, vmem),
         scratch_shapes=[
+            pltpu.VMEM((choices, R), jnp.int32),
+            pltpu.VMEM((choices, R), F32),
+            pltpu.VMEM((1, HD), F32),
+            pltpu.SMEM((1, requests), jnp.int32),
+            pltpu.SMEM((M,), jnp.int32),
             pltpu.VMEM((N, R, W), BF16),
             pltpu.VMEM((rows, W), F32),
             pltpu.VMEM((T, W, FS), BF16),
@@ -315,7 +339,7 @@
             pltpu.VMEM((R, KVF), F32),
             pltpu.VMEM((T, M, KVF), F32),
             pltpu.VMEM((T - 1, M, KVF), F32),
-            dma((6,)), dma((2, T)),
+            dma((11,)), dma((2, T)),
             dma((N,)), dma((N,)),
             dma((requests,)), dma((T, M)),
             dma((T - 1,)), dma((T - 1,)),
@@ -324,10 +348,10 @@
             dma((T - 1,)), dma((T - 1,)),
         ],
         compiler_params=pltpu.CompilerParams(
-            collective_id=0, has_side_effects=True, vmem_limit_bytes=48 * 1024 * 1024
+            collective_id=0, has_side_effects=True, vmem_limit_bytes=64 * 1024 * 1024
         ),
     )(
-        normed, residual, expert_ids, route_weight, w_gate, w_up, w_down, w_kv,
+        normed, residual, expert_ids.T, route_weight.T, w_gate, w_up, w_down, w_kv,
         key_gain.reshape(1, HD), prefill_kv, order, lengths, queries,
     )
     return hidden_state, attention.reshape(M, heads * HD)

time: 37.3 us -> 28.9 us (0.77)
  local copies, waits for them, and re-layouts: 10.3 us -> 2.66 us
  Pallas kernels: 25.3 us -> 24.6 us
    unnamed x20 -> x2, local copies, waits for them, and re-layouts: 10.3 us -> 2.66 us
    pallas_call x1, Pallas kernels: 25.3 us -> 24.6 us  [on_device(): pl.pallas_call(functools.partial(kernel, N, T, R, M, PJ, CTX, KF, FS), ou...]
where the time goes in v2:
time: 28.9 us; the launch traced here: 28.6 us
  Pallas kernels  24.6 us (85%)
  local copies, waits for them, and re-layouts  2.66 us (9%)
  between operations  1.29 us (4%)
    pallas_call x1, Pallas kernels, on_device(): pl.pallas_call(functools.partial(kernel, N, T, R, M, PJ, CTX, KF, FS), ou...  24.6 us
    unnamed x2, local copies, waits for them, and re-layouts  2.66 us

profile of v2, /device:TPU:0, one launch (start us, length us, event | category | flops | bytes accessed | tf_op | source)
XLA Modules:
  0.0 28.6 jit_solution(14384120096668600342)
XLA Ops:
  1.3 24.6 %shard_map.140 = (bf16[4,1024]{1,0:T(4,128)(2,1)}, bf16[1,64,128]{2,1,0:T(8,128)(2,1)}) custom-call(bf16[4,1024]{1,0:T(4,128)(2,1)} %x_hbm.1, bf16[4,1024]{1,0:T(4,128)(2,1)} %res_hbm.1, s32[2,4]{1,0:T(2,128)} %bitcast.9, f32[2,4]{1,0:T(2,128)} %bitcast.10, bf16[1,1024,1024]{2,1,0:T(8,128)(2,1)} %wg_hbm.1, bf16[1,1024,1024]{2,1,0:T(8,128)(2,1)} %wu_hbm.1, ...), custom_call_target="tpu_custom_call" | custom-call | tf_op jit(solution)/shard_map/pallas_call | solution.py:307
  25.9 1.4 %copy.17 = bf16[1,1,64,128]{3,1,2,0:T(2,128)(2,1)} copy(bf16[1,1,64,128]{3,2,1,0:T(8,128)(2,1)} %bitcast.8) | data formatting | bytes 32768
  27.3 1.3 %copy.20 = bf16[4,1024]{1,0:T(4,128)(2,1)} copy(bf16[4,1024]{1,0:T(4,128)(2,1)} %get-tuple-element.8) | data formatting | bytes 16384

commit v3 on v2

--- a/solution.py
+++ b/solution.py
@@ -32,8 +32,8 @@
     hid_ref, att_ref,
     ids_ref, rw_ref, gain_ref, order_ref, len_ref,
     xbuf, xs, wg_v, wu_v, wd_v, wkv_v, res_v, q_v, qs, kv_v, abuf, cbuf,
-    sbuf, rbuf, ibuf, rs, obuf, ebuf, fs, fbuf, frecv,
-    lsem, wsem, xs_s, xs_r, c_s, c_r, g_s, g_r, i_s, i_r, e_s, e_r, f_s, f_r,
+    sbuf, rbuf, ibuf, rs, obuf, ebuf, wsend, wrecv, ws, rp, ps, pbuf, precv,
+    lsem, wsem, xs_s, xs_r, c_s, c_r, g_s, g_r, i_s, i_r, e_s, e_r, w_s, w_r, f_s, f_r,
 ):
     group = lax.axis_index("groups")
     me = lax.axis_index("ep")
@@ -84,28 +84,38 @@
     load_k.start()
 
     barrier = pltpu.get_barrier_semaphore()
-    for j in range(1, N):
-        pl.semaphore_signal(barrier, inc=1, device_id=dev(nexts[j], mt), device_id_type=MESH)
-    for k in range(T - 1):
-        pl.semaphore_signal(barrier, inc=1, device_id=dev(me, peers[k]), device_id_type=MESH)
-    expected = N - 1 + T - 1
-    for m in range(M):
-        p = (mt * M + m) // PJ
-        for t in range(T):
-            @pl.when(jnp.logical_not((p == me) & (mt == t)))
-            def _():
-                pl.semaphore_signal(barrier, inc=1, device_id=dev(p, t), device_id_type=MESH)
-    for j in range(PJ):
-        expected = expected + N - jnp.where((me * PJ + j) // M == mt, 1, 0)
-
+    for j in range(N):
+        for k in range(T):
+            if j or k < T - 1:
+                pl.semaphore_signal(
+                    barrier, inc=1, device_id=dev(nexts[j], peers[k]), device_id_type=MESH
+                )
     load_x.wait()
-    pl.semaphore_wait(barrier, expected)
-
-    dispatch = []
+    pl.semaphore_wait(barrier, N * T - 1)
+
+    dispatch, shares = [], []
     for j in range(1, N):
         c = remote(xbuf.at[0], xbuf.at[j], xs_s.at[j], xs_r.at[j], nexts[j], mt)
         c.start()
         dispatch.append(c)
+
+    load_i.wait()
+    load_s.wait()
+    share = rw_ref[...] / jnp.sum(rw_ref[...], axis=0, keepdims=True)
+    diagonal = lax.broadcasted_iota(jnp.int32, (R, R), 0) == lax.broadcasted_iota(
+        jnp.int32, (R, R), 1
+    )
+
+    def weight_of(e):
+        row = jnp.sum(jnp.where(ids_ref[...] == e, share, F32(0.0)), axis=0, keepdims=True)
+        return jnp.sum(jnp.where(diagonal, row, F32(0.0)), axis=1, keepdims=True)
+
+    for e in range(N):
+        wsend[e] = jnp.broadcast_to(weight_of(e), (R, HD))
+    for j in range(1, N):
+        c = remote(wsend.at[nexts[j]], wrecv.at[j], w_s.at[j], w_r.at[j], nexts[j], mt)
+        c.start()
+        shares.append(c)
 
     def cache_copy(d, j):
         place = me * PJ + j
@@ -176,6 +186,14 @@
         c.start()
         gather.append(c)
 
+    load_r.wait()
+    residual = res_v[...].astype(F32)
+    for c in shares:
+        c.wait_recv()
+    for e in range(N):
+        rp[e * R : (e + 1) * R, :] = jnp.where(me == e, residual, F32(0.0))
+        slot = lax.rem(me - e + N, N)
+        ws[e * R : (e + 1) * R, :] = jnp.where(me == e, wsend[me], wrecv[jnp.maximum(slot, 1)])
     load_d.wait()
 
     def down(k):
@@ -186,7 +204,25 @@
     for k in range(T - 2, -1, -1):
         gather[k].wait_recv()
         total = total + down(k)
+    total = total.astype(BF16).astype(F32)
     rs[...] = total
+    load_k.wait()
+    terms = (rp[...] + ws[:, :1] * total).astype(BF16)
+    total = jnp.dot(terms, wkv_v[...], preferred_element_type=F32)
+    ps[...] = total
+    for i in range(N * T):
+        pbuf[i] = ps[i * M : (i + 1) * M, :]
+    sums = []
+    for j in range(N - 1, -1, -1):
+        for k in range(T):
+            if j or k < T - 1:
+                i = j * T + k
+                c = remote(
+                    pbuf.at[nexts[j] * T + peers[k]], precv.at[i], f_s.at[i], f_r.at[i],
+                    nexts[j], peers[k],
+                )
+                c.start()
+                sums.append((i, c))
     for d in range(N):
         obuf[d] = rs[d * R : (d + 1) * R, :].astype(BF16)
     back = []
@@ -221,40 +257,19 @@
                 jnp.dot(weights.astype(BF16), values, preferred_element_type=F32),
             ))
 
-    load_i.wait()
-    load_s.wait()
-    share = rw_ref[...] / jnp.sum(rw_ref[...], axis=0, keepdims=True)
-    diagonal = lax.broadcasted_iota(jnp.int32, (R, R), 0) == lax.broadcasted_iota(
-        jnp.int32, (R, R), 1
-    )
-
-    def weight_of(e):
-        row = jnp.sum(jnp.where(ids_ref[...] == e, share, F32(0.0)), axis=0, keepdims=True)
-        return jnp.sum(jnp.where(diagonal, row, F32(0.0)), axis=1, keepdims=True)
-
-    load_r.wait()
     mixed = res_v[...].astype(F32)
     for j in range(N):
         if j:
             back[j - 1].wait_recv()
         e = lax.rem(me - j + N, N)
         block = ebuf[j] if j else obuf[me]
-        mixed = mixed + weight_of(e) * block.astype(F32)
-    hidden = mixed.astype(BF16)
-    hid_ref[...] = hidden
-    load_k.wait()
-    fs[...] = jnp.dot(hidden, wkv_v[...], preferred_element_type=F32)
-    for t in range(T):
-        fbuf[t] = fs[t * M : (t + 1) * M, :]
-    sums = []
-    for k in range(T - 1):
-        c = remote(fbuf.at[peers[k]], frecv.at[k], f_s.at[k], f_r.at[k], me, peers[k])
-        c.start()
-        sums.append(c)
-    fresh = fbuf[mt]
-    for k in range(T - 2, -1, -1):
-        sums[k].wait_recv()
-        fresh = fresh + frecv[k]
+        mixed = mixed + wsend[e][:, :1] * block.astype(F32)
+    hid_ref[...] = mixed.astype(BF16)
+    fresh = pbuf[me * T + mt]
+    for i, c in sums:
+        c.wait_recv()
+    for i, c in sums:
+        fresh = fresh + precv[i]
     fresh = fresh.astype(BF16).astype(F32)
 
     for m in range(M):
@@ -274,7 +289,7 @@
             out = (summed * old + new * value) / (weight * old + new)
             att_ref[m, g * QG : (g + 1) * QG, :] = out.astype(BF16)
 
-    for c in dispatch + scatter + gather + back + sums:
+    for c in dispatch + shares + scatter + gather + back + [c for _, c in sums]:
         c.wait_send()
     for d in range(N):
         for j in range(PJ):
@@ -336,16 +351,21 @@
             pltpu.VMEM((rows, W), F32),
             pltpu.VMEM((N, R, W), BF16),
             pltpu.VMEM((N, R, W), BF16),
-            pltpu.VMEM((R, KVF), F32),
-            pltpu.VMEM((T, M, KVF), F32),
-            pltpu.VMEM((T - 1, M, KVF), F32),
+            pltpu.VMEM((N, R, HD), F32),
+            pltpu.VMEM((N, R, HD), F32),
+            pltpu.VMEM((rows, HD), F32),
+            pltpu.VMEM((rows, W), F32),
+            pltpu.VMEM((rows, KVF), F32),
+            pltpu.VMEM((N * T, M, KVF), F32),
+            pltpu.VMEM((N * T, M, KVF), F32),
             dma((11,)), dma((2, T)),
             dma((N,)), dma((N,)),
             dma((requests,)), dma((T, M)),
             dma((T - 1,)), dma((T - 1,)),
             dma((T - 1,)), dma((T - 1,)),
             dma((N,)), dma((N,)),
-            dma((T - 1,)), dma((T - 1,)),
+            dma((N,)), dma((N,)),
+            dma((N * T,)), dma((N * T,)),
         ],
         compiler_params=pltpu.CompilerParams(
             collective_id=0, has_side_effects=True, vmem_limit_bytes=64 * 1024 * 1024

time: 28.9 us -> 27.7 us (0.958)
  Pallas kernels: 24.6 us -> 23.4 us
    pallas_call x1, Pallas kernels: 24.6 us -> 23.4 us  [on_device(): pl.pallas_call(functools.partial(kernel, N, T, R, M, PJ, CTX, KF, FS), ou...]
where the time goes in v3:
time: 27.7 us; the launch traced here: 27.3 us
  Pallas kernels  23.4 us (84%)
  local copies, waits for them, and re-layouts  2.66 us (10%)
  between operations  1.29 us (5%)
    pallas_call x1, Pallas kernels, on_device(): pl.pallas_call(functools.partial(kernel, N, T, R, M, PJ, CTX, KF, FS), ou...  23.4 us
    unnamed x2, local copies, waits for them, and re-layouts  2.66 us

profile of v3, /device:TPU:0, one launch (start us, length us, event | category | flops | bytes accessed | tf_op | source)
XLA Modules:
  0.0 27.3 jit_solution(3576147795625710616)
XLA Ops:
  1.3 23.4 %shard_map.140 = (bf16[4,1024]{1,0:T(4,128)(2,1)}, bf16[1,64,128]{2,1,0:T(8,128)(2,1)}) custom-call(bf16[4,1024]{1,0:T(4,128)(2,1)} %x_hbm.1, bf16[4,1024]{1,0:T(4,128)(2,1)} %res_hbm.1, s32[2,4]{1,0:T(2,128)} %bitcast.9, f32[2,4]{1,0:T(2,128)} %bitcast.10, bf16[1,1024,1024]{2,1,0:T(8,128)(2,1)} %wg_hbm.1, bf16[1,1024,1024]{2,1,0:T(8,128)(2,1)} %wu_hbm.1, ...), custom_call_target="tpu_custom_call" | custom-call | tf_op jit(solution)/shard_map/pallas_call | solution.py:322
  24.6 1.4 %copy.17 = bf16[1,1,64,128]{3,1,2,0:T(2,128)(2,1)} copy(bf16[1,1,64,128]{3,2,1,0:T(8,128)(2,1)} %bitcast.8) | data formatting | bytes 32768
  26.0 1.3 %copy.20 = bf16[4,1024]{1,0:T(4,128)(2,1)} copy(bf16[4,1024]{1,0:T(4,128)(2,1)} %get-tuple-element.8) | data formatting | bytes 16384

commit v4 on v3

--- a/solution.py
+++ b/solution.py
@@ -141,6 +141,25 @@
             def _():
                 c.start()
 
+    for c in dispatch:
+        c.wait_recv()
+    for e in range(N):
+        slot = lax.rem(me - e + N, N)
+        xs[e * R : (e + 1) * R, :] = xbuf[slot].astype(F32)
+    x = xs[...].astype(BF16)
+
+    scatter = []
+    for k in range(T):
+        load_w[k][0].wait()
+        gate = jnp.dot(x, wg_v[k], preferred_element_type=F32)
+        load_w[k][1].wait()
+        up = jnp.dot(x, wu_v[k], preferred_element_type=F32)
+        if k < T - 1:
+            sbuf[k, :, :FS] = gate.astype(BF16)
+            sbuf[k, :, FS:] = up.astype(BF16)
+            c = remote(sbuf.at[k], rbuf.at[k], g_s.at[k], g_r.at[k], me, peers[k])
+            c.start()
+            scatter.append(c)
     load_q.wait()
     load_l.wait()
     load_g.wait()
@@ -156,25 +175,6 @@
         sine = jnp.sin(angle)
         turns.append((jnp.cos(angle), jnp.where(lane < HD // 2, -sine, sine)))
 
-    for c in dispatch:
-        c.wait_recv()
-    for e in range(N):
-        slot = lax.rem(me - e + N, N)
-        xs[e * R : (e + 1) * R, :] = xbuf[slot].astype(F32)
-    x = xs[...].astype(BF16)
-
-    scatter = []
-    for k in range(T):
-        load_w[k][0].wait()
-        gate = jnp.dot(x, wg_v[k], preferred_element_type=F32)
-        load_w[k][1].wait()
-        up = jnp.dot(x, wu_v[k], preferred_element_type=F32)
-        if k < T - 1:
-            sbuf[k, :, :FS] = gate.astype(BF16)
-            sbuf[k, :, FS:] = up.astype(BF16)
-            c = remote(sbuf.at[k], rbuf.at[k], g_s.at[k], g_r.at[k], me, peers[k])
-            c.start()
-            scatter.append(c)
     for k in range(T - 2, -1, -1):
         scatter[k].wait_recv()
         gate = gate + rbuf[k, :, :FS].astype(F32)
@@ -368,11 +368,18 @@
             dma((N * T,)), dma((N * T,)),
         ],
         compiler_params=pltpu.CompilerParams(
-            collective_id=0, has_side_effects=True, vmem_limit_bytes=64 * 1024 * 1024
+            collective_id=0, has_side_effects=True, vmem_limit_bytes=48 * 1024 * 1024
         ),
     )(
-        normed, residual, expert_ids.T, route_weight.T, w_gate, w_up, w_down, w_kv,
-        key_gain.reshape(1, HD), prefill_kv, order, lengths, queries,
+        *[
+            pltpu.with_memory_space_constraint(value, pltpu.HBM)
+            for value in (
+                normed, residual, expert_ids.T, route_weight.T, w_gate, w_up, w_down, w_kv,
+                key_gain.reshape(1, HD), prefill_kv, order,
+            )
+        ],
+        lengths,
+        pltpu.with_memory_space_constraint(queries, pltpu.HBM),
     )
     return hidden_state, attention.reshape(M, heads * HD)
 

time: 27.7 us -> 25.5 us (0.921)
  local copies, waits for them, and re-layouts: 2.66 us -> 1.24 us
  Pallas kernels: 23.4 us -> 22.7 us
    unnamed x2, local copies, waits for them, and re-layouts: 2.66 us -> 1.24 us
    pallas_call x1, Pallas kernels: 23.4 us -> 22.7 us  [on_device(): pl.pallas_call(functools.partial(kernel, N, T, R, M, PJ, CTX, KF, FS), ou...]
where the time goes in v4:
time: 25.5 us; the launch traced here: 25.3 us
  Pallas kernels  22.7 us (89%)
  between operations  1.29 us (5%)
  local copies, waits for them, and re-layouts  1.24 us (5%)
    pallas_call x1, Pallas kernels, on_device(): pl.pallas_call(functools.partial(kernel, N, T, R, M, PJ, CTX, KF, FS), ou...  22.7 us
    unnamed x2, local copies, waits for them, and re-layouts  1.24 us

profile of v4, /device:TPU:0, one launch (start us, length us, event | category | flops | bytes accessed | tf_op | source)
XLA Modules:
  0.0 25.3 jit_solution(9964137147437178975)
XLA Ops:
  1.3 22.7 %shard_map.140 = (bf16[4,1024]{1,0:T(4,128)(2,1)S(1)}, bf16[1,64,128]{2,1,0:T(8,128)(2,1)S(1)}) custom-call(bf16[4,1024]{1,0:T(4,128)(2,1)} %x_hbm.1, bf16[4,1024]{1,0:T(4,128)(2,1)} %res_hbm.1, s32[2,4]{1,0:T(2,128)} %bitcast.9, f32[2,4]{1,0:T(2,128)} %bitcast.10, bf16[1,1024,1024]{2,1,0:T(8,128)(2,1)} %wg_hbm.1, bf16[1,1024,1024]{2,1,0:T(8,128)(2,1)} %wu_hbm.1, ...), custom_call_target="tpu_custom_call" | custom-call | tf_op jit(solution)/shard_map/pallas_call | solution.py:322
  24.0 0.6 %copy.17 = bf16[1,1,64,128]{3,1,2,0:T(2,128)(2,1)} copy(bf16[1,1,64,128]{3,2,1,0:T(8,128)(2,1)S(1)} %bitcast.7) | data formatting | bytes 32768
  24.7 0.6 %copy.20 = bf16[4,1024]{1,0:T(4,128)(2,1)} copy(bf16[4,1024]{1,0:T(4,128)(2,1)S(1)} %get-tuple-element.8) | data formatting | bytes 16384

commit v5 on v4

--- a/solution.py
+++ b/solution.py
@@ -90,15 +90,6 @@
                 pl.semaphore_signal(
                     barrier, inc=1, device_id=dev(nexts[j], peers[k]), device_id_type=MESH
                 )
-    load_x.wait()
-    pl.semaphore_wait(barrier, N * T - 1)
-
-    dispatch, shares = [], []
-    for j in range(1, N):
-        c = remote(xbuf.at[0], xbuf.at[j], xs_s.at[j], xs_r.at[j], nexts[j], mt)
-        c.start()
-        dispatch.append(c)
-
     load_i.wait()
     load_s.wait()
     share = rw_ref[...] / jnp.sum(rw_ref[...], axis=0, keepdims=True)
@@ -112,6 +103,15 @@
 
     for e in range(N):
         wsend[e] = jnp.broadcast_to(weight_of(e), (R, HD))
+    load_x.wait()
+    pl.semaphore_wait(barrier, N * T - 1)
+
+    dispatch, shares = [], []
+    for j in range(1, N):
+        c = remote(xbuf.at[0], xbuf.at[j], xs_s.at[j], xs_r.at[j], nexts[j], mt)
+        c.start()
+        dispatch.append(c)
+
     for j in range(1, N):
         c = remote(wsend.at[nexts[j]], wrecv.at[j], w_s.at[j], w_r.at[j], nexts[j], mt)
         c.start()

time: 25.5 us -> 25.4 us (level)
  no operation moved by 1% of the time
where the time goes in v5:
time: 25.4 us; the launch traced here: 25.3 us
  Pallas kernels  22.7 us (89%)
  between operations  1.29 us (5%)
  local copies, waits for them, and re-layouts  1.24 us (5%)
    pallas_call x1, Pallas kernels, on_device(): pl.pallas_call(functools.partial(kernel, N, T, R, M, PJ, CTX, KF, FS), ou...  22.7 us
    unnamed x2, local copies, waits for them, and re-layouts  1.24 us

profile of v5, /device:TPU:0, one launch (start us, length us, event | category | flops | bytes accessed | tf_op | source)
XLA Modules:
  0.0 25.3 jit_solution(9413224805541511963)
XLA Ops:
  1.3 22.7 %shard_map.140 = (bf16[4,1024]{1,0:T(4,128)(2,1)S(1)}, bf16[1,64,128]{2,1,0:T(8,128)(2,1)S(1)}) custom-call(bf16[4,1024]{1,0:T(4,128)(2,1)} %x_hbm.1, bf16[4,1024]{1,0:T(4,128)(2,1)} %res_hbm.1, s32[2,4]{1,0:T(2,128)} %bitcast.9, f32[2,4]{1,0:T(2,128)} %bitcast.10, bf16[1,1024,1024]{2,1,0:T(8,128)(2,1)} %wg_hbm.1, bf16[1,1024,1024]{2,1,0:T(8,128)(2,1)} %wu_hbm.1, ...), custom_call_target="tpu_custom_call" | custom-call | tf_op jit(solution)/shard_map/pallas_call | solution.py:322
  24.0 0.6 %copy.17 = bf16[1,1,64,128]{3,1,2,0:T(2,128)(2,1)} copy(bf16[1,1,64,128]{3,2,1,0:T(8,128)(2,1)S(1)} %bitcast.7) | data formatting | bytes 32768
  24.7 0.6 %copy.20 = bf16[4,1024]{1,0:T(4,128)(2,1)} copy(bf16[4,1024]{1,0:T(4,128)(2,1)S(1)} %get-tuple-element.8) | data formatting | bytes 16384
